TPU v7x, 256 devices: a whole 4x4x8 slice. The times are simulated.
256 devices in a mesh: energy: 128 (over y, z_lo, x, core), slab: 2 (over z_hi).
Axes of the slice: x: 4, y: 4, z: 8 (z_hi: 2, z_lo: 4; z = z_hi * 4 + z_lo), core: 2. Of those that a mesh axis runs over, the one named last changes fastest.
Arguments:
- green_ret: bfloat16 [384, 4, 3, 2, 192, 192], P('energy', 'slab'), may hold values from -0.3125 to 0.3125
- sigma_less: bfloat16 [384, 4, 2, 192, 192], P('energy', 'slab'), may hold values from -6 to 6
- screened: float32 [384, 4, 2, 36864], P(None, 'slab', None, 'energy'), may hold values from -4 to 4
Outputs:
- sigma_new: bfloat16 [384, 4, 2, 192, 192], P('energy', 'slab')
- renewed: bfloat16 [384, 4, 2, 192, 192], P('energy', 'slab')
All inputs are finite; a program needn't handle non-finite values.
Results may differ from a plain program's by a relative error of at most 0.0085.
Values may be sent and summed in bfloat16 or wider, within the bound.
A program may use at most 128 MiB of HBM per device.

v0:
```python
import functools
import math

import jax
import jax.numpy as jnp
import numpy as np
from jax import lax
from jax.experimental import pallas as pl
from jax.experimental.pallas import tpu as pltpu
from jax.sharding import PartitionSpec as P

MESH = pl.DeviceIdType.MESH
F32, BF16 = jnp.float32, jnp.bfloat16
E, B = 384, 192
CHIPS, PER_CHIP, OWN = 64, 6, 3
ROWS, PITCH = 54, 56
HALF = B * 3 // 2
SCALE = 1.0 / (E * math.sqrt(E))


def tables():
    point = np.arange(E)
    held = np.array([PER_CHIP * c + k for k in range(PER_CHIP) for c in range(CHIPS)])

    def parts(rows, cols):
        angle = (rows[:, None] * cols[None, :] % E) * (2.0 * np.pi / E)
        return np.cos(angle), np.sin(angle)

    cos, sin = parts(point, point)
    whole = np.concatenate([np.concatenate([cos, sin], 1), np.concatenate([-sin, cos], 1)], 0)
    there = np.concatenate(parts(point, held), 1)
    back = np.concatenate(parts(held, point), 1)
    return [t.astype(np.float32).astype(BF16) for t in (whole, there, back)]


def nn(a, b):
    return lax.dot_general(a, b, (((1,), (0,)), ((), ())), preferred_element_type=F32)


def nt(a, b):
    return lax.dot_general(a, b, (((1,), (1,)), ((), ())), preferred_element_type=F32)


def adjoint_product(ar, ai, br, bi):
    return (nt(ar, br) + nt(ai, bi)).astype(BF16), (nt(ai, br) - nt(ar, bi)).astype(BF16)


def product(ar, ai, br, bi):
    return nn(ar, br) - nn(ai, bi), nn(ar, bi) + nn(ai, br)


def unpack(row):
    return (
        jnp.concatenate([row[:, :128], row[:, 256:320]], axis=1),
        jnp.concatenate([row[:, 128:256], row[:, 320:384]], axis=1),
    )


def place(i, k, e):
    return (i * 3 + k) * PER_CHIP + e


def kernel(
    g_hbm, s_hbm, w_hbm, tw_hbm, tf_hbm, tb_hbm, new_ref, ren_ref,
    g, s, w, tw, tf, tb, wall, wsend, what, hsend, hrecv, lsend, lrecv, lf, m,
    out1, in1, x, pb, out2, in2, nsend, nrecv, load, local, send, recv,
):
    me, sl = lax.axis_index("energy"), lax.axis_index("slab")
    chip, core = me // 2, me % 2
    sib = me + 1 - 2 * core
    sign = jnp.where(lax.broadcasted_iota(jnp.int32, (1, 128), 1) < 64, 1.0, -1.0).astype(F32)

    loads = [
        pltpu.make_async_copy(src, dst, load.at[n])
        for n, (src, dst) in enumerate(((s_hbm, s), (g_hbm, g), (w_hbm, w), (tw_hbm, tw), (tf_hbm, tf), (tb_hbm, tb)))
    ]
    for copy in loads:
        copy.start()

    barrier = pltpu.get_barrier_semaphore()
    pl.semaphore_signal(barrier, inc=1, device_id=(me, 1 - sl), device_id_type=MESH)
    pl.semaphore_signal(barrier, inc=1, device_id=(sib, sl), device_id_type=MESH)

    @pl.loop(1, CHIPS)
    def _(n):
        pl.semaphore_signal(barrier, inc=1, device_id=((me + 2 * n) % 128, sl), device_id_type=MESH)

    def remote(src, dst, n, to):
        return pltpu.make_async_remote_copy(
            src_ref=src, dst_ref=dst, send_sem=send.at[n], recv_sem=recv.at[n], device_id=to, device_id_type=MESH
        )

    def spread(src, dst, n):
        @pl.loop(0, CHIPS)
        def _(j):
            dz, dx, dy = (j + 2) % 4, (j + j // 4 + 2) % 4, (j + j // 16 + 2) % 4
            to = ((chip // 16 + dy) % 4) * 16 + ((chip // 4 + dz) % 4) * 4 + (chip + dx) % 4

            @pl.when(to != chip)
            def _():
                remote(src.at[to], dst.at[chip], n, (2 * to + core, sl)).start()

        pltpu.make_async_copy(src.at[chip], dst.at[chip], local.at[n]).start()

    def spread_sent(src, n):
        some = src.at[pl.ds(0, CHIPS - 1)]
        pltpu.make_async_copy(some, some, send.at[n]).wait()

    def spread_here(src, dst, n):
        some = dst.at[pl.ds(0, CHIPS - 1)]
        pltpu.make_async_copy(some, some, recv.at[n]).wait()
        pltpu.make_async_copy(src.at[chip], dst.at[chip], local.at[n]).wait()

    edge = 1 - sl
    loads[0].wait()

    @pl.loop(0, OWN)
    def _(e):
        sr, si = s[e, edge, 0], s[e, edge, 1]
        hsend[e, :, 0:128] = sr[:, :128]
        hsend[e, :, 128:256] = si[:, :128]
        hsend[e, :, 256:320] = sr[:, 128:]
        hsend[e, :, 320:384] = si[:, 128:]

    pl.semaphore_wait(barrier, CHIPS + 1)
    halo = remote(hsend, hrecv, 0, (me, 1 - sl))
    halo.start()

    loads[2].wait()
    mine = wall.at[pl.ds(pl.multiple_of(core * HALF, 32), HALF)]
    mine[:, :E] = w[core, 0].astype(BF16)
    mine[:, E:] = w[core, 1].astype(BF16)
    wsend[:, :E] = w[1 - core, 0].astype(BF16)
    wsend[:, E:] = w[1 - core, 1].astype(BF16)
    swap_w = remote(wsend, mine, 1, (sib, sl))
    swap_w.start()

    loads[1].wait()

    def term(e, slab, j, sr, si):
        gr, gi = g[e, slab, j, 0], g[e, slab, j, 1]
        ir, ii = adjoint_product(sr, si, gr, gi)
        return product(gr, gi, ir, ii)

    def lesser(slab, with_halo):
        holder = slab == core

        @pl.loop(0, OWN)
        def _(e):
            lr, li = term(e, slab, 1, s[e, slab, 0], s[e, slab, 1])
            tr, ti = term(e, slab, 2 - 2 * slab, s[e, 1 - slab, 0], s[e, 1 - slab, 1])
            lr, li = lr + tr, li + ti
            if with_halo:
                tr, ti = term(e, slab, 2 * slab, *unpack(hrecv[e]))
                lr, li = lr + tr, li + ti
            at = OWN * core + e
            lf[at, 0] = lr[:, :128]
            lf[at, 1] = li[:, :128]
            lf[at, 2, :, 0:64] = lr[:, 128:]
            lf[at, 2, :, 64:128] = li[:, 128:]

        @pl.when(jnp.logical_not(holder))
        def _():
            @pl.loop(0, OWN)
            def _(e):
                for k in range(3):
                    lsend[e, :, 128 * k : 128 * k + 128] = lf[OWN * core + e, k].astype(BF16)

            remote(lsend, lrecv, 2, (sib, sl)).start()

        @pl.when(holder)
        def _():
            pltpu.make_async_copy(lrecv, lrecv, recv.at[2]).wait()

            @pl.loop(0, OWN)
            def _(e):
                for k in range(3):
                    lf[OWN * (1 - core) + e, k] = lrecv[e, :, 128 * k : 128 * k + 128].astype(F32)

            for e in range(PER_CHIP):
                for i in range(3):
                    for k in range(3):
                        m[pl.ds(place(i, k, e), CHIPS, stride=PITCH), :] = lf[e, k, pl.ds(i, CHIPS, stride=3), :]

            @pl.loop(0, CHIPS)
            def _(c):
                out1[c] = m[pl.ds(pl.multiple_of(c * PITCH, 8), ROWS), :].astype(BF16)

            spread(out1, in1, 3)

    lesser(sl, False)

    swap_w.wait()
    loads[3].wait()
    for i in range(3):
        full = nt(tw[...], wall[B * i : B * i + B, :]) * SCALE
        what[0, i] = full[:E, :128]
        what[1, i] = full[E:, :128]
        what[2, i, :, 0:64] = full[:E, 128:]
        what[2, i, :, 64:128] = full[:E, 128:]
        what[3, i, :, 0:64] = -full[E:, 128:]
        what[3, i, :, 64:128] = full[E:, 128:]

    halo.wait()
    lesser(edge, True)

    loads[4].wait()
    loads[5].wait()
    spread_here(out1, in1, 3)

    @pl.loop(0, CHIPS)
    def _(c):
        m[pl.ds(pl.multiple_of(c * PITCH, 8), ROWS), :] = in1[c].astype(F32)

    for e in range(PER_CHIP):
        top, low = slice(CHIPS * e, CHIPS * e + CHIPS), slice(E + CHIPS * e, E + CHIPS * e + CHIPS)
        for i in range(3):
            at = 384 * i
            a, b, c = (m[pl.ds(place(i, k, e), CHIPS, stride=PITCH), :] for k in range(3))
            x[top, at : at + 128] = a.astype(BF16)
            x[low, at : at + 128] = b.astype(BF16)
            x[top, at + 128 : at + 256] = b.astype(BF16)
            x[low, at + 128 : at + 256] = (-a).astype(BF16)
            x[top, at + 256 : at + 384] = c.astype(BF16)
            x[low, at + 256 : at + 384] = (pltpu.roll(c, 64, 1) * sign).astype(BF16)

    for i in range(3):
        ghat = nn(tf[...], x[:, 384 * i : 384 * i + 384])
        gr, gi, gm = ghat[:, :128], ghat[:, 128:256], ghat[:, 256:]
        wr, wi = what[0, i], what[1, i]
        pr = gr * wr - gi * wi
        pi = gr * wi + gi * wr
        pm = gm * what[2, i] + pltpu.roll(gm, 64, 1) * what[3, i]
        pb[:E, 0:128] = pr.astype(BF16)
        pb[E:, 0:128] = (-pi).astype(BF16)
        pb[:E, 128:256] = pi.astype(BF16)
        pb[E:, 128:256] = pr.astype(BF16)
        pb[:E, 256:384] = pm.astype(BF16)
        pb[E:, 256:384] = (pltpu.roll(pm, 64, 1) * -sign).astype(BF16)
        fresh = nn(tb[...], pb[...])
        for e in range(PER_CHIP):
            for k in range(3):
                m[pl.ds(place(i, k, e), CHIPS, stride=PITCH), :] = fresh[CHIPS * e : CHIPS * e + CHIPS, 128 * k : 128 * k + 128]

    @pl.loop(0, CHIPS)
    def _(c):
        out2[c] = m[pl.ds(pl.multiple_of(c * PITCH, 8), ROWS), :].astype(BF16)

    spread(out2, in2, 4)
    spread_here(out2, in2, 4)

    @pl.loop(0, CHIPS)
    def _(c):
        m[pl.ds(pl.multiple_of(c * PITCH, 8), ROWS), :] = in2[c].astype(F32)

    for e in range(PER_CHIP):
        for i in range(3):
            for k in range(3):
                lf[e, k, pl.ds(i, CHIPS, stride=3), :] = m[pl.ds(place(i, k, e), CHIPS, stride=PITCH), :]

    @pl.loop(0, OWN)
    def _(e):
        for k in range(3):
            nsend[e, :, 128 * k : 128 * k + 128] = lf[OWN * (1 - core) + e, k].astype(BF16)

    swap_n = remote(nsend, nrecv, 5, (sib, sl))
    swap_n.start()

    def second(e, slab, sr, si):
        new_ref[e, slab, 0] = sr
        new_ref[e, slab, 1] = si
        rr, ri = term(e, slab, 1, sr, si)
        ren_ref[e, slab, 0] = rr.astype(BF16)
        ren_ref[e, slab, 1] = ri.astype(BF16)

    @pl.loop(0, OWN)
    def _(e):
        at = OWN * core + e
        tail = lf[at, 2].astype(BF16)
        second(
            e, core,
            jnp.concatenate([lf[at, 0].astype(BF16), tail[:, :64]], axis=1),
            jnp.concatenate([lf[at, 1].astype(BF16), tail[:, 64:]], axis=1),
        )

    swap_n.wait()

    @pl.loop(0, OWN)
    def _(e):
        second(e, 1 - core, *unpack(nrecv[e]))

    pltpu.make_async_copy(lsend, lsend, send.at[2]).wait()
    spread_sent(out1, 3)
    spread_sent(out2, 4)


def shards(green_ret, sigma_less, screened):
    out = jax.ShapeDtypeStruct(sigma_less.shape, BF16)
    packed = pltpu.VMEM((OWN, B, 2 * B), BF16)
    box = pltpu.VMEM((CHIPS, ROWS, 128), BF16)
    return pl.pallas_call(
        kernel,
        out_shape=(out, out),
        in_specs=[pl.BlockSpec(memory_space=pl.ANY)] * 6,
        out_specs=[pl.BlockSpec(memory_space=pltpu.VMEM)] * 2,
        scratch_shapes=[
            pltpu.VMEM(green_ret.shape, BF16),
            pltpu.VMEM(sigma_less.shape, BF16),
            pltpu.VMEM((2, 2, HALF, E), F32),
            pltpu.VMEM((2 * E, 2 * E), BF16),
            pltpu.VMEM((E, 2 * E), BF16),
            pltpu.VMEM((E, 2 * E), BF16),
            pltpu.VMEM((2 * HALF, 2 * E), BF16),
            pltpu.VMEM((HALF, 2 * E), BF16),
            pltpu.VMEM((4, 3, E, 128), F32),
            packed, packed, packed, packed,
            pltpu.VMEM((PER_CHIP, 3, B, 128), F32),
            pltpu.VMEM((CHIPS * PITCH, 128), F32),
            box, box,
            pltpu.VMEM((2 * E, 1152), BF16),
            pltpu.VMEM((2 * E, 384), BF16),
            box, box, packed, packed,
            pltpu.SemaphoreType.DMA((6,)),
            pltpu.SemaphoreType.DMA((6,)),
            pltpu.SemaphoreType.DMA((6,)),
            pltpu.SemaphoreType.DMA((6,)),
        ],
        compiler_params=pltpu.CompilerParams(collective_id=0, has_side_effects=True, vmem_limit_bytes=50 * 2**20),
        name="wire",
    )(green_ret, sigma_less, jnp.transpose(screened, (1, 2, 3, 0)), *tables())


def solution(mesh):
    in_specs = (
        P("energy", "slab", None, None, None, None),
        P("energy", "slab", None, None, None),
        P(None, "slab", None, "energy"),
    )
    out_specs = (P("energy", "slab", None, None, None), P("energy", "slab", None, None, None))
    return jax.shard_map(shards, mesh=mesh, in_specs=in_specs, out_specs=out_specs, check_vma=False)
```

profile of v0, /device:TPU:1, one launch (start us, length us, event | category | flops | bytes accessed | tf_op | source)
XLA Modules:
  0.0 88.1 jit_solution(16396141792915882401)
XLA Ops:
  0.6 0.0 copy-start
  0.6 1.1 %copy-done = bf16[384,768]{1,0:T(8,128)(2,1)S(1)} copy-done((bf16[384,768]{1,0:T(8,128)(2,1)S(1)}, bf16[384,768]{1,0:T(8,128)(2,1)}, u32[]{:S(2)}) %copy-start) | copy-done | bytes 589848
  1.7 0.0 copy-start.1
  1.7 1.1 %copy-done.1 = bf16[384,768]{1,0:T(8,128)(2,1)S(1)} copy-done((bf16[384,768]{1,0:T(8,128)(2,1)S(1)}, bf16[384,768]{1,0:T(8,128)(2,1)}, u32[]{:S(2)}) %copy-start.1) | copy-done | bytes 589848
  2.8 83.3 %wire.1 = (bf16[3,2,2,192,192]{4,3,2,1,0:T(8,128)(2,1)S(1)}, bf16[3,2,2,192,192]{4,3,2,1,0:T(8,128)(2,1)S(1)}) custom-call(bf16[3,2,3,2,192,192]{5,4,3,2,1,0:T(8,128)(2,1)} %g_hbm.1, bf16[3,2,2,192,192]{4,3,2,1,0:T(8,128)(2,1)} %s_hbm.1, f32[2,2,288,384]{3,2,1,0:T(8,128)} %bitcast.1, bf16[768,768]{1,0:T(8,128)(2,1)} %constant.6.clone.tw_hbm, ...), custom_call_target="tpu_custom_call" | custom-call | tf_op jit(solution)/shard_map/wire/pallas_call | solution.py:301
  86.1 1.0 %copy.10 = bf16[3,2,2,192,192]{4,3,2,1,0:T(8,128)(2,1)} copy(bf16[3,2,2,192,192]{4,3,2,1,0:T(8,128)(2,1)S(1)} %get-tuple-element.4) | data formatting | bytes 1769472
  87.1 1.0 %copy.11 = bf16[3,2,2,192,192]{4,3,2,1,0:T(8,128)(2,1)} copy(bf16[3,2,2,192,192]{4,3,2,1,0:T(8,128)(2,1)S(1)} %get-tuple-element.5) | data formatting | bytes 1769472
Async XLA Ops:
  0.6 1.1 %copy-start = (bf16[384,768]{1,0:T(8,128)(2,1)S(1)}, bf16[384,768]{1,0:T(8,128)(2,1)}, u32[]{:S(2)}) copy-start(bf16[384,768]{1,0:T(8,128)(2,1)} %constant.8.clone.tb_hbm) | copy-start | bytes 1769476
  1.7 1.1 %copy-start.1 = (bf16[384,768]{1,0:T(8,128)(2,1)S(1)}, bf16[384,768]{1,0:T(8,128)(2,1)}, u32[]{:S(2)}) copy-start(bf16[384,768]{1,0:T(8,128)(2,1)} %constant.7.clone.tf_hbm) | copy-start | bytes 1769476
where the time goes:
time: 88.3 us; the launch traced here: 88.1 us
  Pallas kernels  83.3 us (94%)
  local copies, waits for them, and re-layouts  4.15 us (5%)
    pallas_call x1, Pallas kernels, shards(): pl.pallas_call(kernel, out_shape=(out, out), in_specs=[pl.BlockSpec(memor...  83.3 us
    unnamed x6, local copies, waits for them, and re-layouts  4.15 us

commit v1 on v0

v1 whole, which is shorter than its diff:
```python
import functools
import math

import jax
import jax.numpy as jnp
import numpy as np
from jax import lax
from jax.experimental import pallas as pl
from jax.experimental.pallas import tpu as pltpu
from jax.sharding import PartitionSpec as P

MESH = pl.DeviceIdType.MESH
F32, BF16 = jnp.float32, jnp.bfloat16
E, B = 384, 192
CHIPS, PER_CHIP, OWN = 64, 6, 3
ROWS, PITCH = 54, 56
HALF = B * 3 // 2
HALO, LESSER, NEW, SCREEN, THERE, BACK, COPIES = 0, 3, 6, 9, 10, 11, 12
SCALE = 1.0 / (E * math.sqrt(E))


def tables():
    point = np.arange(E)

    def parts(rows, cols):
        angle = (rows[:, None] * cols[None, :] % E) * (2.0 * np.pi / E)
        return np.cos(angle), np.sin(angle)

    def held(core):
        own = [(OWN * core + q) % PER_CHIP for q in range(PER_CHIP)]
        return np.array([PER_CHIP * c + k for k in own for c in range(CHIPS)])

    cos, sin = parts(point, point)
    whole = np.concatenate([np.concatenate([cos, sin], 1), np.concatenate([-sin, cos], 1)], 0)
    there = np.stack([np.concatenate(parts(point, held(core)), 1) for core in range(2)])
    back = np.stack([np.concatenate(parts(held(core), point), 1) for core in range(2)])
    return [t.astype(np.float32).astype(BF16) for t in (whole, there, back)]


def nn(a, b):
    return lax.dot_general(a, b, (((1,), (0,)), ((), ())), preferred_element_type=F32)


def nt(a, b):
    return lax.dot_general(a, b, (((1,), (1,)), ((), ())), preferred_element_type=F32)


def adjoint_product(ar, ai, br, bi):
    return (nt(ar, br) + nt(ai, bi)).astype(BF16), (nt(ai, br) - nt(ar, bi)).astype(BF16)


def product(ar, ai, br, bi):
    return nn(ar, br) - nn(ai, bi), nn(ar, bi) + nn(ai, br)


def unpack(row):
    return (
        jnp.concatenate([row[:, :128], row[:, 256:320]], axis=1),
        jnp.concatenate([row[:, 128:256], row[:, 320:384]], axis=1),
    )


def place(i, k, e):
    return (i * 3 + k) * PER_CHIP + e


def kernel(
    g_hbm, s, w_hbm, tw_hbm, tf_hbm, tb_hbm, new_ref, ren_ref,
    g, w, tw, tf, tb, wall, wsend, what, hsend, hrecv, lsend, lrecv, part, lf, m,
    out1, in1, x, pb, out2, in2, nsend, nrecv, load, local, send, recv, line,
):
    me, sl = lax.axis_index("energy"), lax.axis_index("slab")
    chip, core = me // 2, me % 2
    py, pz, px = chip // 16, (chip // 4) % 4, chip % 4
    sib = me + 1 - 2 * core
    sign = jnp.where(lax.broadcasted_iota(jnp.int32, (1, 128), 1) < 64, 1.0, -1.0).astype(F32)

    def at(dy, dz, dx):
        return ((py + dy) % 4) * 16 + ((pz + dz) % 4) * 4 + (px + dx) % 4

    def signal(sem, device, slab):
        pl.semaphore_signal(sem, inc=1, device_id=(device, slab), device_id_type=MESH)

    barrier = pltpu.get_barrier_semaphore()
    signal(barrier, me, 1 - sl)
    signal(barrier, sib, sl)
    for d in range(1, 4):
        for off in ((0, 0, d), (d, 0, 0), (0, d, 0)):
            signal(barrier, 2 * at(*off) + core, sl)

    loads = [
        pltpu.make_async_copy(src, dst, load.at[n])
        for n, (src, dst) in enumerate(
            ((g_hbm, g), (w_hbm, w), (tw_hbm, tw), (tf_hbm.at[core], tf), (tb_hbm.at[core], tb))
        )
    ]
    for copy in loads:
        copy.start()

    def remote(src, dst, n, to):
        return pltpu.make_async_remote_copy(
            src_ref=src, dst_ref=dst, send_sem=send.at[n], recv_sem=recv.at[n], device_id=to, device_id_type=MESH
        )

    def arrived(dst, n):
        pltpu.make_async_copy(dst, dst, recv.at[n]).wait()

    def sent(src, n):
        pltpu.make_async_copy(src, src, send.at[n]).wait()

    def spread(src, dst, n):
        def message(to):
            src[to] = m[pl.ds(pl.multiple_of(to * PITCH, 8), ROWS), :].astype(BF16)

        for dz in (2, 1, 3, 0):
            @pl.loop(0 if dz else 1, 16)
            def _(j):
                to = at(j // 4, dz, j + j // 4)
                message(to)
                remote(src.at[to], dst.at[chip], n, (2 * to + core, sl)).start()

        message(chip)
        pltpu.make_async_copy(src.at[chip], dst.at[chip], local.at[n]).start()

    def collect(src, dst, n):
        arrived(dst.at[pl.ds(0, CHIPS - 1)], n)
        pltpu.make_async_copy(src.at[chip], dst.at[chip], local.at[n]).wait()

        @pl.loop(0, CHIPS)
        def _(c):
            m[pl.ds(pl.multiple_of(c * PITCH, 8), ROWS), :] = dst[c].astype(F32)

    def pack(dst, re, im):
        dst[:, 0:128] = re[:, :128].astype(BF16)
        dst[:, 128:256] = im[:, :128].astype(BF16)
        dst[:, 256:320] = re[:, 128:].astype(BF16)
        dst[:, 320:384] = im[:, 128:].astype(BF16)

    edge = 1 - sl

    @pl.loop(0, OWN)
    def _(e):
        pack(hsend.at[e], s[e, edge, 0], s[e, edge, 1])

    pl.semaphore_wait(barrier, 11)
    halo = [remote(hsend.at[e], hrecv.at[e], HALO + e, (me, 1 - sl)) for e in range(OWN)]
    for copy in halo:
        copy.start()
    for d in range(1, 4):
        signal(line.at[0], 2 * at(0, 0, d) + core, sl)

    loads[1].wait()
    mine = wall.at[pl.ds(pl.multiple_of(core * HALF, 32), HALF)]
    mine[:, :E] = w[core, 0].astype(BF16)
    mine[:, E:] = w[core, 1].astype(BF16)
    wsend[:, :E] = w[1 - core, 0].astype(BF16)
    wsend[:, E:] = w[1 - core, 1].astype(BF16)
    swap_w = remote(wsend, mine, SCREEN, (sib, sl))
    swap_w.start()
    pl.semaphore_wait(line.at[0], 3)
    for d in range(1, 4):
        signal(line.at[1], 2 * at(d, 0, 0) + core, sl)

    loads[0].wait()

    def term(e, slab, j, sr, si):
        gr, gi = g[e, slab, j, 0], g[e, slab, j, 1]
        ir, ii = adjoint_product(sr, si, gr, gi)
        return product(gr, gi, ir, ii)

    def inside(e, slab):
        lr, li = term(e, slab, 1, s[e, slab, 0], s[e, slab, 1])
        tr, ti = term(e, slab, 2 - 2 * slab, s[e, 1 - slab, 0], s[e, 1 - slab, 1])
        return lr + tr, li + ti

    def deliver(e, slab, lr, li):
        @pl.when(slab == core)
        def _():
            lf[e, 0] = lr[:, :128]
            lf[e, 1] = li[:, :128]
            lf[e, 2, :, 0:64] = lr[:, 128:]
            lf[e, 2, :, 64:128] = li[:, 128:]
            gather(e)

        @pl.when(slab != core)
        def _():
            pack(lsend.at[e], lr, li)
            remote(lsend.at[e], lrecv.at[e], LESSER + e, (sib, sl)).start()

    def gather(q):
        for i in range(3):
            for k in range(3):
                m[pl.ds(place(i, k, q), CHIPS, stride=PITCH), :] = lf[q, k, pl.ds(i, CHIPS, stride=3), :]

    def receive(e):
        arrived(lrecv.at[e], LESSER + e)
        for k in range(3):
            lf[OWN + e, k] = lrecv[e, :, 128 * k : 128 * k + 128].astype(F32)
        gather(OWN + e)

    for e in range(OWN):
        deliver(e, sl, *inside(e, sl))

    @pl.loop(0, OWN)
    def _(e):
        part[e, 0], part[e, 1] = inside(e, edge)

    pl.semaphore_wait(line.at[1], 3)

    swap_w.wait()
    loads[2].wait()
    for i in range(3):
        full = nt(tw[...], wall[B * i : B * i + B, :]) * SCALE
        what[0, i] = full[:E, :128]
        what[1, i] = full[E:, :128]
        what[2, i, :, 0:64] = full[:E, 128:]
        what[2, i, :, 64:128] = full[:E, 128:]
        what[3, i, :, 0:64] = -full[E:, 128:]
        what[3, i, :, 64:128] = full[E:, 128:]

    @pl.when(core == sl)
    def _():
        for e in range(OWN):
            receive(e)

    for e in range(OWN):
        halo[e].wait()
        tr, ti = term(e, edge, 2 * edge, *unpack(hrecv[e]))
        deliver(e, edge, part[e, 0] + tr, part[e, 1] + ti)

        if e == 1:
            @pl.when(core == sl)
            def _():
                spread(out1, in1, THERE)

    @pl.when(core == edge)
    def _():
        for e in range(OWN):
            receive(e)
        spread(out1, in1, THERE)

    loads[3].wait()
    loads[4].wait()
    collect(out1, in1, THERE)

    for q in range(PER_CHIP):
        top, low = slice(CHIPS * q, CHIPS * q + CHIPS), slice(E + CHIPS * q, E + CHIPS * q + CHIPS)
        for i in range(3):
            a, b, c = (m[pl.ds(place(i, k, q), CHIPS, stride=PITCH), :] for k in range(3))
            x[top, 384 * i : 384 * i + 128] = a.astype(BF16)
            x[low, 384 * i : 384 * i + 128] = b.astype(BF16)
            x[top, 384 * i + 128 : 384 * i + 256] = b.astype(BF16)
            x[low, 384 * i + 128 : 384 * i + 256] = (-a).astype(BF16)
            x[top, 384 * i + 256 : 384 * i + 384] = c.astype(BF16)
            x[low, 384 * i + 256 : 384 * i + 384] = (pltpu.roll(c, 64, 1) * sign).astype(BF16)

    for i in range(3):
        ghat = nn(tf[...], x[:, 384 * i : 384 * i + 384])
        gr, gi, gm = ghat[:, :128], ghat[:, 128:256], ghat[:, 256:]
        wr, wi = what[0, i], what[1, i]
        pr = gr * wr - gi * wi
        pi = gr * wi + gi * wr
        pm = gm * what[2, i] + pltpu.roll(gm, 64, 1) * what[3, i]
        pb[:E, 0:128] = pr.astype(BF16)
        pb[E:, 0:128] = (-pi).astype(BF16)
        pb[:E, 128:256] = pi.astype(BF16)
        pb[E:, 128:256] = pr.astype(BF16)
        pb[:E, 256:384] = pm.astype(BF16)
        pb[E:, 256:384] = (pltpu.roll(pm, 64, 1) * -sign).astype(BF16)
        fresh = nn(tb[...], pb[...])
        for q in range(PER_CHIP):
            for k in range(3):
                m[pl.ds(place(i, k, q), CHIPS, stride=PITCH), :] = fresh[CHIPS * q : CHIPS * q + CHIPS, 128 * k : 128 * k + 128]

    spread(out2, in2, BACK)
    collect(out2, in2, BACK)

    def restore(q):
        for i in range(3):
            for k in range(3):
                lf[q, k, pl.ds(i, CHIPS, stride=3), :] = m[pl.ds(place(i, k, q), CHIPS, stride=PITCH), :]

    def second(e, slab, sr, si):
        new_ref[e, slab, 0] = sr
        new_ref[e, slab, 1] = si
        rr, ri = term(e, slab, 1, sr, si)
        ren_ref[e, slab, 0] = rr.astype(BF16)
        ren_ref[e, slab, 1] = ri.astype(BF16)

    swap_n = [remote(nsend.at[e], nrecv.at[e], NEW + e, (sib, sl)) for e in range(OWN)]
    for e in range(OWN):
        restore(OWN + e)
        for k in range(3):
            nsend[e, :, 128 * k : 128 * k + 128] = lf[OWN + e, k].astype(BF16)
        swap_n[e].start()

    for e in range(OWN):
        restore(e)
        tail = lf[e, 2].astype(BF16)
        second(
            e, core,
            jnp.concatenate([lf[e, 0].astype(BF16), tail[:, :64]], axis=1),
            jnp.concatenate([lf[e, 1].astype(BF16), tail[:, 64:]], axis=1),
        )

    for e in range(OWN):
        swap_n[e].wait()
        second(e, 1 - core, *unpack(nrecv[e]))

    for e in range(OWN):
        sent(lsend.at[e], LESSER + e)
    sent(out1.at[pl.ds(0, CHIPS - 1)], THERE)
    sent(out2.at[pl.ds(0, CHIPS - 1)], BACK)


def shards(green_ret, sigma_less, screened):
    out = jax.ShapeDtypeStruct(sigma_less.shape, BF16)
    packed = pltpu.VMEM((OWN, B, 2 * B), BF16)
    box = pltpu.VMEM((CHIPS, ROWS, 128), BF16)
    return pl.pallas_call(
        kernel,
        out_shape=(out, out),
        in_specs=[pl.BlockSpec(memory_space=pltpu.VMEM if n == 1 else pltpu.HBM) for n in range(6)],
        out_specs=[pl.BlockSpec(memory_space=pltpu.VMEM)] * 2,
        scratch_shapes=[
            pltpu.VMEM(green_ret.shape, BF16),
            pltpu.VMEM((2, 2, HALF, E), F32),
            pltpu.VMEM((2 * E, 2 * E), BF16),
            pltpu.VMEM((E, 2 * E), BF16),
            pltpu.VMEM((E, 2 * E), BF16),
            pltpu.VMEM((2 * HALF, 2 * E), BF16),
            pltpu.VMEM((HALF, 2 * E), BF16),
            pltpu.VMEM((4, 3, E, 128), F32),
            packed, packed, packed, packed,
            pltpu.VMEM((OWN, 2, B, B), F32),
            pltpu.VMEM((PER_CHIP, 3, B, 128), F32),
            pltpu.VMEM((CHIPS * PITCH, 128), F32),
            box, box,
            pltpu.VMEM((2 * E, 1152), BF16),
            pltpu.VMEM((2 * E, 384), BF16),
            box, box, packed, packed,
            pltpu.SemaphoreType.DMA((5,)),
            pltpu.SemaphoreType.DMA((COPIES,)),
            pltpu.SemaphoreType.DMA((COPIES,)),
            pltpu.SemaphoreType.DMA((COPIES,)),
            pltpu.SemaphoreType.REGULAR((2,)),
        ],
        compiler_params=pltpu.CompilerParams(collective_id=0, has_side_effects=True, vmem_limit_bytes=50 * 2**20),
        name="wire",
    )(green_ret, sigma_less, jnp.transpose(screened, (1, 2, 3, 0)), *tables())


def solution(mesh):
    in_specs = (
        P("energy", "slab", None, None, None, None),
        P("energy", "slab", None, None, None),
        P(None, "slab", None, "energy"),
    )
    out_specs = (P("energy", "slab", None, None, None), P("energy", "slab", None, None, None))
    return jax.shard_map(shards, mesh=mesh, in_specs=in_specs, out_specs=out_specs, check_vma=False)
```

time: 88.3 us -> 84.9 us (0.961)
  the two profiles are of different devices: /device:TPU:1 before, /device:TPU:67 now
where the time goes in v1:
time: 84.9 us; the launch traced here: 84.7 us
  Pallas kernels  80.8 us (95%)
  local copies, waits for them, and re-layouts  3.29 us (4%)
    pallas_call x1, Pallas kernels, shards(): pl.pallas_call(kernel, out_shape=(out, out), in_specs=[pl.BlockSpec(memor...  80.8 us
    unnamed x4, local copies, waits for them, and re-layouts  3.29 us

profile of v1, /device:TPU:67, one launch (start us, length us, event | category | flops | bytes accessed | tf_op | source)
XLA Modules:
  0.0 84.7 jit_solution(4473731994438517461)
XLA Ops:
  0.6 0.0 copy-start
  0.6 1.3 %copy-done = bf16[3,2,2,192,192]{4,3,2,1,0:T(8,128)(2,1)S(1)} copy-done((bf16[3,2,2,192,192]{4,3,2,1,0:T(8,128)(2,1)S(1)}, bf16[3,2,2,192,192]{4,3,2,1,0:T(8,128)(2,1)}, u32[]{:S(2)}) %copy-start) | copy-done | bytes 884760
  1.9 80.8 %wire.1 = (bf16[3,2,2,192,192]{4,3,2,1,0:T(8,128)(2,1)S(1)}, bf16[3,2,2,192,192]{4,3,2,1,0:T(8,128)(2,1)S(1)}) custom-call(bf16[3,2,3,2,192,192]{5,4,3,2,1,0:T(8,128)(2,1)} %g_hbm.1, bf16[3,2,2,192,192]{4,3,2,1,0:T(8,128)(2,1)S(1)} %copy-done, f32[2,2,288,384]{3,2,1,0:T(8,128)} %bitcast.1, bf16[768,768]{1,0:T(8,128)(2,1)} %constant.6.clone.tw_hbm, ...), custom_call_target="tpu_custom_call" | custom-call | tf_op jit(solution)/shard_map/wire/pallas_call | solution.py:320
  82.7 1.0 %copy.10 = bf16[3,2,2,192,192]{4,3,2,1,0:T(8,128)(2,1)} copy(bf16[3,2,2,192,192]{4,3,2,1,0:T(8,128)(2,1)S(1)} %get-tuple-element.4) | data formatting | bytes 1769472
  83.7 1.0 %copy.11 = bf16[3,2,2,192,192]{4,3,2,1,0:T(8,128)(2,1)} copy(bf16[3,2,2,192,192]{4,3,2,1,0:T(8,128)(2,1)S(1)} %get-tuple-element.5) | data formatting | bytes 1769472
Async XLA Ops:
  0.6 1.3 %copy-start = (bf16[3,2,2,192,192]{4,3,2,1,0:T(8,128)(2,1)S(1)}, bf16[3,2,2,192,192]{4,3,2,1,0:T(8,128)(2,1)}, u32[]{:S(2)}) copy-start(bf16[3,2,2,192,192]{4,3,2,1,0:T(8,128)(2,1)} %s.1) | copy-start | bytes 2654212

commit v2 on v1

v2 whole, which is shorter than its diff:
```python
import functools
import math

import jax
import jax.numpy as jnp
import numpy as np
from jax import lax
from jax.experimental import pallas as pl
from jax.experimental.pallas import tpu as pltpu
from jax.sharding import PartitionSpec as P

MESH = pl.DeviceIdType.MESH
F32, BF16 = jnp.float32, jnp.bfloat16
E, B = 384, 192
CHIPS, PER_CHIP, OWN = 64, 6, 3
PITCH = 32
SETS = (((0, 0), (0, 1), (0, 2), (1, 2)), ((1, 0), (1, 1), (2, 0), (2, 1), (2, 2)))
HALF = B * 3 // 2
HALO, LESSER, NEW, SCREEN, THERE, BACK, COPIES = 0, 3, 9, 15, 17, 19, 21
EARLY = 1
SCALE = 1.0 / (E * math.sqrt(E))


def tables():
    point = np.arange(E)

    def parts(rows, cols):
        angle = (rows[:, None] * cols[None, :] % E) * (2.0 * np.pi / E)
        return np.cos(angle), np.sin(angle)

    def held(core):
        own = [(OWN * core + q) % PER_CHIP for q in range(PER_CHIP)]
        return np.array([PER_CHIP * c + k for k in own for c in range(CHIPS)])

    cos, sin = parts(point, point)
    whole = np.concatenate([np.concatenate([cos, sin], 1), np.concatenate([-sin, cos], 1)], 0)
    there = np.stack([np.concatenate(parts(point, held(core)), 1) for core in range(2)])
    back = np.stack([np.concatenate(parts(held(core), point), 1) for core in range(2)])
    return [t.astype(np.float32).astype(BF16) for t in (whole, there, back)]


def nn(a, b):
    return lax.dot_general(a, b, (((1,), (0,)), ((), ())), preferred_element_type=F32)


def nt(a, b):
    return lax.dot_general(a, b, (((1,), (1,)), ((), ())), preferred_element_type=F32)


def adjoint_product(ar, ai, br, bi):
    return (nt(ar, br) + nt(ai, bi)).astype(BF16), (nt(ai, br) - nt(ar, bi)).astype(BF16)


def product(ar, ai, br, bi):
    return nn(ar, br) - nn(ai, bi), nn(ar, bi) + nn(ai, br)


def unpack(row):
    return (
        jnp.concatenate([row[:, :128], row[:, 256:320]], axis=1),
        jnp.concatenate([row[:, 128:256], row[:, 320:384]], axis=1),
    )


def comb(t, q):
    return pl.ds(t * PER_CHIP + q, CHIPS, stride=PITCH)


def kernel(
    g_hbm, s, w_hbm, tw_hbm, tf_hbm, tb_hbm, new_ref, ren_ref,
    g, w, tw, tf, tb, wall, what, hsend, hrecv, part, lf, x, pb,
    m0, m1, ls0, ls1, lr0, lr1, out0, out1, in0, in1, bout0, bout1, bin0, bin1, ns0, ns1, nr0, nr1,
    load, local, send, recv, line,
):
    me, sl = lax.axis_index("energy"), lax.axis_index("slab")
    chip, core = me // 2, me % 2
    py, pz, px = chip // 16, (chip // 4) % 4, chip % 4
    sib = me + 1 - 2 * core
    m, ls, lr, out, inn = (m0, m1), (ls0, ls1), (lr0, lr1), (out0, out1), (in0, in1)
    bout, bin, ns, nr = (bout0, bout1), (bin0, bin1), (ns0, ns1), (nr0, nr1)
    sign = jnp.where(lax.broadcasted_iota(jnp.int32, (1, 128), 1) < 64, 1.0, -1.0).astype(F32)

    def at(dy, dz, dx):
        return ((py + dy) % 4) * 16 + ((pz + dz) % 4) * 4 + (px + dx) % 4

    def signal(sem, device, slab):
        pl.semaphore_signal(sem, inc=1, device_id=(device, slab), device_id_type=MESH)

    barrier = pltpu.get_barrier_semaphore()
    signal(barrier, me, 1 - sl)
    signal(barrier, sib, sl)
    for d in range(1, 4):
        for off in ((0, 0, d), (d, 0, 0), (0, d, 0)):
            signal(barrier, 2 * at(*off) + core, sl)

    loads = [
        pltpu.make_async_copy(src, dst, load.at[n])
        for n, (src, dst) in enumerate(
            ((g_hbm, g), (w_hbm, w), (tw_hbm, tw), (tf_hbm.at[core], tf), (tb_hbm.at[core], tb))
        )
    ]
    for copy in loads:
        copy.start()

    def remote(src, dst, n, to):
        return pltpu.make_async_remote_copy(
            src_ref=src, dst_ref=dst, send_sem=send.at[n], recv_sem=recv.at[n], device_id=to, device_id_type=MESH
        )

    def arrived(dst, n):
        pltpu.make_async_copy(dst, dst, recv.at[n]).wait()

    def sent(src, n):
        pltpu.make_async_copy(src, src, send.at[n]).wait()

    def each(stage, do):
        for c in range(2):
            @pl.when(core == c)
            def _():
                do(c ^ stage)

    def spread(t, src, dst, n):
        rows = src.shape[1]

        def message(to):
            src[to] = m[t][pl.ds(pl.multiple_of(to * PITCH, 8), rows), :].astype(BF16)

        for dz in (2, 1, 3, 0):
            @pl.loop(0 if dz else 1, 16)
            def _(j):
                to = at(j // 4, dz, j + j // 4)
                message(to)
                remote(src.at[to], dst.at[chip], n, (2 * to + core, sl)).start()

        message(chip)
        pltpu.make_async_copy(src.at[chip], dst.at[chip], local.at[n]).start()

    def collect(t, src, dst, n):
        arrived(dst.at[pl.ds(0, CHIPS - 1)], n)
        pltpu.make_async_copy(src.at[chip], dst.at[chip], local.at[n]).wait()

        @pl.loop(0, CHIPS)
        def _(c):
            m[t][pl.ds(pl.multiple_of(c * PITCH, 8), dst.shape[1]), :] = dst[c].astype(F32)

    def pack(dst, re, im):
        dst[:, 0:128] = re[:, :128].astype(BF16)
        dst[:, 128:256] = im[:, :128].astype(BF16)
        dst[:, 256:320] = re[:, 128:].astype(BF16)
        dst[:, 320:384] = im[:, 128:].astype(BF16)

    edge = 1 - sl

    @pl.loop(0, OWN)
    def _(e):
        pack(hsend.at[e], s[e, edge, 0], s[e, edge, 1])

    pl.semaphore_wait(barrier, 11)
    halo = [remote(hsend.at[e], hrecv.at[e], HALO + e, (me, 1 - sl)) for e in range(OWN)]
    for copy in halo:
        copy.start()
    for d in range(1, 4):
        signal(line.at[0], 2 * at(0, 0, d) + core, sl)

    loads[1].wait()
    swap_w = []
    for slab in range(2):
        mine = wall.at[slab, pl.ds(pl.multiple_of(core * HALF, 32), HALF)]
        mine[:, :E] = w[slab, 0].astype(BF16)
        mine[:, E:] = w[slab, 1].astype(BF16)
        swap_w.append(remote(mine, mine, SCREEN + slab, (sib, sl)))
        swap_w[slab].start()
    pl.semaphore_wait(line.at[0], 3)
    for d in range(1, 4):
        signal(line.at[1], 2 * at(d, 0, 0) + core, sl)

    loads[0].wait()

    def term(e, slab, j, sr, si):
        gr, gi = g[e, slab, j, 0], g[e, slab, j, 1]
        ir, ii = adjoint_product(sr, si, gr, gi)
        return product(gr, gi, ir, ii)

    def inside(e, slab):
        lr, li = term(e, slab, 1, s[e, slab, 0], s[e, slab, 1])
        tr, ti = term(e, slab, 2 - 2 * slab, s[e, 1 - slab, 0], s[e, 1 - slab, 1])
        return lr + tr, li + ti

    def scatter(e, re, im):
        lf[e, 0] = re[:, :128]
        lf[e, 1] = im[:, :128]
        lf[e, 2, :, 0:64] = re[:, 128:]
        lf[e, 2, :, 64:128] = im[:, 128:]

    def deliver(stage, e):
        def do(mine):
            for t, (i, k) in enumerate(SETS[mine]):
                m[mine][comb(t, e), :] = lf[e, k, pl.ds(i, CHIPS, stride=3), :]
            other = 1 - mine
            for t, (i, k) in enumerate(SETS[other]):
                ls[other][e, t] = lf[e, k, pl.ds(i, CHIPS, stride=3), :].astype(BF16)
            remote(ls[other].at[e], lr[other].at[e], LESSER + OWN * other + e, (sib, sl)).start()

        each(stage, do)

    def receive(mine):
        for e in range(OWN):
            arrived(lr[mine].at[e], LESSER + OWN * mine + e)
            for t in range(len(SETS[mine])):
                m[mine][comb(t, OWN + e), :] = lr[mine][e, t].astype(F32)

    def send_there(mine):
        spread(mine, out[mine], inn[mine], THERE + mine)

    for e in range(OWN):
        scatter(e, *inside(e, sl))
        deliver(0, e)

    @pl.loop(0, OWN)
    def _(e):
        part[e, 0], part[e, 1] = inside(e, edge)

    pl.semaphore_wait(line.at[1], 3)

    for copy in swap_w:
        copy.wait()
    loads[2].wait()
    slab_of = ((sl + core) % 2, (sl + core + 1) % 2)

    def pairs(i, full):
        what[0, i] = full[:E, :128]
        what[1, i] = full[E:, :128]

    def tail(i, full):
        what[2, i, :, 0:64] = full[:E]
        what[2, i, :, 64:128] = full[:E]
        what[3, i, :, 0:64] = -full[E:]
        what[3, i, :, 64:128] = full[E:]

    def transform(c, lo, hi):
        return nt(tw[...], wall[slab_of[c], lo:hi, :]) * SCALE

    for c, i in ((0, 0), (1, 2)):
        full = transform(c, B * i, B * i + B)
        pairs(i, full)
        tail(i, full[:, 128:])
    pairs(1, transform(1, B, B + 128))
    tail(1, transform(0, B + 128, 2 * B))

    each(0, receive)
    for e in range(OWN):
        halo[e].wait()
        tr, ti = term(e, edge, 2 * edge, *unpack(hrecv[e]))
        scatter(e, part[e, 0] + tr, part[e, 1] + ti)
        deliver(1, e)
        if e == EARLY:
            each(0, send_there)

    each(1, receive)
    each(1, send_there)

    loads[3].wait()
    loads[4].wait()

    def convolve(mine):
        collect(mine, out[mine], inn[mine], THERE + mine)
        tiles = SETS[mine]
        wide = 128 * len(tiles)
        lanes = [slice(128 * t, 128 * t + 128) for t in range(len(tiles))]
        for q in range(PER_CHIP):
            top, low = slice(CHIPS * q, CHIPS * q + CHIPS), slice(E + CHIPS * q, E + CHIPS * q + CHIPS)
            for t, (i, k) in enumerate(tiles):
                a = m[mine][comb(t, q), :]
                x[top, lanes[t]] = a.astype(BF16)
                if k == 0:
                    x[low, lanes[t + 1]] = (-a).astype(BF16)
                elif k == 1:
                    x[low, lanes[t - 1]] = a.astype(BF16)
                else:
                    x[low, lanes[t]] = (pltpu.roll(a, 64, 1) * sign).astype(BF16)

        ghat = nn(tf[...], x[:, :wide])
        for t, (i, k) in enumerate(tiles):
            if k == 0:
                gr, gi = ghat[:, lanes[t]], ghat[:, lanes[t + 1]]
                wr, wi = what[0, i], what[1, i]
                pr = gr * wr - gi * wi
                pi = gr * wi + gi * wr
                pb[:E, lanes[t]] = pr.astype(BF16)
                pb[E:, lanes[t]] = (-pi).astype(BF16)
                pb[:E, lanes[t + 1]] = pi.astype(BF16)
                pb[E:, lanes[t + 1]] = pr.astype(BF16)
            elif k == 2:
                gm = ghat[:, lanes[t]]
                pm = gm * what[2, i] + pltpu.roll(gm, 64, 1) * what[3, i]
                pb[:E, lanes[t]] = pm.astype(BF16)
                pb[E:, lanes[t]] = (pltpu.roll(pm, 64, 1) * -sign).astype(BF16)
        fresh = nn(tb[...], pb[:, :wide])
        for q in range(PER_CHIP):
            for t in range(len(tiles)):
                m[mine][comb(t, q), :] = fresh[CHIPS * q : CHIPS * q + CHIPS, lanes[t]]
        spread(mine, bout[mine], bin[mine], BACK + mine)

    each(0, convolve)
    each(1, convolve)

    def second(e, slab):
        last = lf[e, 2].astype(BF16)
        sr = jnp.concatenate([lf[e, 0].astype(BF16), last[:, :64]], axis=1)
        si = jnp.concatenate([lf[e, 1].astype(BF16), last[:, 64:]], axis=1)
        new_ref[e, slab, 0] = sr
        new_ref[e, slab, 1] = si
        rr, ri = term(e, slab, 1, sr, si)
        ren_ref[e, slab, 0] = rr.astype(BF16)
        ren_ref[e, slab, 1] = ri.astype(BF16)

    for stage, slab in ((0, sl), (1, edge)):
        def give(mine):
            collect(mine, bout[mine], bin[mine], BACK + mine)
            for e in range(OWN):
                for t in range(len(SETS[mine])):
                    ns[mine][e, t] = m[mine][comb(t, OWN + e), :].astype(BF16)
                remote(ns[mine].at[e], nr[mine].at[e], NEW + OWN * mine + e, (sib, sl)).start()
            for e in range(OWN):
                for t, (i, k) in enumerate(SETS[mine]):
                    lf[e, k, pl.ds(i, CHIPS, stride=3), :] = m[mine][comb(t, e), :]

        def take(mine):
            other = 1 - mine
            for e in range(OWN):
                arrived(nr[other].at[e], NEW + OWN * other + e)
                for t, (i, k) in enumerate(SETS[other]):
                    lf[e, k, pl.ds(i, CHIPS, stride=3), :] = nr[other][e, t].astype(F32)

        each(stage, give)
        each(stage, take)
        for e in range(OWN):
            second(e, slab)

    for t in range(2):
        for e in range(OWN):
            sent(ls[t].at[e], LESSER + OWN * t + e)
            sent(ns[t].at[e], NEW + OWN * t + e)
        sent(out[t].at[pl.ds(0, CHIPS - 1)], THERE + t)
        sent(bout[t].at[pl.ds(0, CHIPS - 1)], BACK + t)


def shards(green_ret, sigma_less, screened):
    out = jax.ShapeDtypeStruct(sigma_less.shape, BF16)
    packed = pltpu.VMEM((OWN, B, 2 * B), BF16)

    def both(make):
        return [make(len(tiles)) for tiles in SETS]

    def tiles(n):
        return pltpu.VMEM((OWN, n, CHIPS, 128), BF16)

    def box(n):
        return pltpu.VMEM((CHIPS, n * PER_CHIP, 128), BF16)

    return pl.pallas_call(
        kernel,
        out_shape=(out, out),
        in_specs=[pl.BlockSpec(memory_space=pltpu.VMEM if n == 1 else pltpu.HBM) for n in range(6)],
        out_specs=[pl.BlockSpec(memory_space=pltpu.VMEM)] * 2,
        scratch_shapes=[
            pltpu.VMEM(green_ret.shape, BF16),
            pltpu.VMEM((2, 2, HALF, E), F32),
            pltpu.VMEM((2 * E, 2 * E), BF16),
            pltpu.VMEM((E, 2 * E), BF16),
            pltpu.VMEM((E, 2 * E), BF16),
            pltpu.VMEM((2, 2 * HALF, 2 * E), BF16),
            pltpu.VMEM((4, 3, E, 128), F32),
            packed, packed,
            pltpu.VMEM((OWN, 2, B, B), F32),
            pltpu.VMEM((OWN, 3, B, 128), F32),
            pltpu.VMEM((2 * E, 640), BF16),
            pltpu.VMEM((2 * E, 640), BF16),
            *[pltpu.VMEM((CHIPS * PITCH, 128), F32)] * 2,
            *both(tiles), *both(tiles), *both(box), *both(box), *both(box), *both(box), *both(tiles), *both(tiles),
            pltpu.SemaphoreType.DMA((5,)),
            pltpu.SemaphoreType.DMA((COPIES,)),
            pltpu.SemaphoreType.DMA((COPIES,)),
            pltpu.SemaphoreType.DMA((COPIES,)),
            pltpu.SemaphoreType.REGULAR((2,)),
        ],
        compiler_params=pltpu.CompilerParams(collective_id=0, has_side_effects=True, vmem_limit_bytes=50 * 2**20),
        name="wire",
    )(green_ret, sigma_less, jnp.transpose(screened, (1, 2, 3, 0)), *tables())


def solution(mesh):
    in_specs = (
        P("energy", "slab", None, None, None, None),
        P("energy", "slab", None, None, None),
        P(None, "slab", None, "energy"),
    )
    out_specs = (P("energy", "slab", None, None, None), P("energy", "slab", None, None, None))
    return jax.shard_map(shards, mesh=mesh, in_specs=in_specs, out_specs=out_specs, check_vma=False)
```

time: 84.9 us -> 79 us (0.931)
  the two profiles are of different devices: /device:TPU:67 before, /device:TPU:1 now
where the time goes in v2:
time: 79 us; the launch traced here: 78.5 us
  Pallas kernels  74.5 us (94%)
  local copies, waits for them, and re-layouts  3.29 us (4%)
    pallas_call x1, Pallas kernels, shards(): pl.pallas_call(kernel, out_shape=(out, out), in_specs=[pl.BlockSpec(memor...  74.5 us
    unnamed x4, local copies, waits for them, and re-layouts  3.29 us

profile of v2, /device:TPU:1, one launch (start us, length us, event | category | flops | bytes accessed | tf_op | source)
XLA Modules:
  0.0 78.5 jit_solution(3073560649224074624)
XLA Ops:
  0.6 0.0 copy-start
  0.6 1.3 %copy-done = bf16[3,2,2,192,192]{4,3,2,1,0:T(8,128)(2,1)S(1)} copy-done((bf16[3,2,2,192,192]{4,3,2,1,0:T(8,128)(2,1)S(1)}, bf16[3,2,2,192,192]{4,3,2,1,0:T(8,128)(2,1)}, u32[]{:S(2)}) %copy-start) | copy-done | bytes 884760
  1.9 74.5 %wire.1 = (bf16[3,2,2,192,192]{4,3,2,1,0:T(8,128)(2,1)S(1)}, bf16[3,2,2,192,192]{4,3,2,1,0:T(8,128)(2,1)S(1)}) custom-call(bf16[3,2,3,2,192,192]{5,4,3,2,1,0:T(8,128)(2,1)} %g_hbm.1, bf16[3,2,2,192,192]{4,3,2,1,0:T(8,128)(2,1)S(1)} %copy-done, f32[2,2,288,384]{3,2,1,0:T(8,128)} %bitcast.1, bf16[768,768]{1,0:T(8,128)(2,1)} %constant.6.clone.tw_hbm, ...), custom_call_target="tpu_custom_call" | custom-call | tf_op jit(solution)/shard_map/wire/pallas_call | solution.py:361
  76.5 1.0 %copy.10 = bf16[3,2,2,192,192]{4,3,2,1,0:T(8,128)(2,1)} copy(bf16[3,2,2,192,192]{4,3,2,1,0:T(8,128)(2,1)S(1)} %get-tuple-element.4) | data formatting | bytes 1769472
  77.5 1.0 %copy.11 = bf16[3,2,2,192,192]{4,3,2,1,0:T(8,128)(2,1)} copy(bf16[3,2,2,192,192]{4,3,2,1,0:T(8,128)(2,1)S(1)} %get-tuple-element.5) | data formatting | bytes 1769472
Async XLA Ops:
  0.6 1.3 %copy-start = (bf16[3,2,2,192,192]{4,3,2,1,0:T(8,128)(2,1)S(1)}, bf16[3,2,2,192,192]{4,3,2,1,0:T(8,128)(2,1)}, u32[]{:S(2)}) copy-start(bf16[3,2,2,192,192]{4,3,2,1,0:T(8,128)(2,1)} %s.1) | copy-start | bytes 2654212

commit v3 on v2

--- a/solution.py
+++ b/solution.py
@@ -156,9 +156,10 @@
         pack(hsend.at[e], s[e, edge, 0], s[e, edge, 1])
 
     pl.semaphore_wait(barrier, 11)
-    halo = [remote(hsend.at[e], hrecv.at[e], HALO + e, (me, 1 - sl)) for e in range(OWN)]
-    for copy in halo:
-        copy.start()
+    for e in range(OWN):
+        for row in range(0, B, 32):
+            piece = (e, pl.ds(row, 32))
+            remote(hsend.at[piece], hrecv.at[piece], HALO + e, (me, 1 - sl)).start()
     for d in range(1, 4):
         signal(line.at[0], 2 * at(0, 0, d) + core, sl)
 
@@ -249,7 +250,7 @@
 
     each(0, receive)
     for e in range(OWN):
-        halo[e].wait()
+        arrived(hrecv.at[e], HALO + e)
         tr, ti = term(e, edge, 2 * edge, *unpack(hrecv[e]))
         scatter(e, part[e, 0] + tr, part[e, 1] + ti)
         deliver(1, e)
@@ -337,6 +338,8 @@
         for e in range(OWN):
             second(e, slab)
 
+    for e in range(OWN):
+        sent(hsend.at[e], HALO + e)
     for t in range(2):
         for e in range(OWN):
             sent(ls[t].at[e], LESSER + OWN * t + e)

time: 79 us -> 79 us (level)
  no operation moved by 1% of the time
where the time goes in v3:
time: 79 us; the launch traced here: 78.5 us
  Pallas kernels  74.5 us (94%)
  local copies, waits for them, and re-layouts  3.29 us (4%)
    pallas_call x1, Pallas kernels, shards(): pl.pallas_call(kernel, out_shape=(out, out), in_specs=[pl.BlockSpec(memor...  74.5 us
    unnamed x4, local copies, waits for them, and re-layouts  3.29 us

profile of v3, /device:TPU:1, one launch (start us, length us, event | category | flops | bytes accessed | tf_op | source)
XLA Modules:
  0.0 78.5 jit_solution(6333952843177606214)
XLA Ops:
  0.6 0.0 copy-start
  0.6 1.3 %copy-done = bf16[3,2,2,192,192]{4,3,2,1,0:T(8,128)(2,1)S(1)} copy-done((bf16[3,2,2,192,192]{4,3,2,1,0:T(8,128)(2,1)S(1)}, bf16[3,2,2,192,192]{4,3,2,1,0:T(8,128)(2,1)}, u32[]{:S(2)}) %copy-start) | copy-done | bytes 884760
  1.9 74.5 %wire.1 = (bf16[3,2,2,192,192]{4,3,2,1,0:T(8,128)(2,1)S(1)}, bf16[3,2,2,192,192]{4,3,2,1,0:T(8,128)(2,1)S(1)}) custom-call(bf16[3,2,3,2,192,192]{5,4,3,2,1,0:T(8,128)(2,1)} %g_hbm.1, bf16[3,2,2,192,192]{4,3,2,1,0:T(8,128)(2,1)S(1)} %copy-done, f32[2,2,288,384]{3,2,1,0:T(8,128)} %bitcast.1, bf16[768,768]{1,0:T(8,128)(2,1)} %constant.6.clone.tw_hbm, ...), custom_call_target="tpu_custom_call" | custom-call | tf_op jit(solution)/shard_map/wire/pallas_call | solution.py:364
  76.5 1.0 %copy.10 = bf16[3,2,2,192,192]{4,3,2,1,0:T(8,128)(2,1)} copy(bf16[3,2,2,192,192]{4,3,2,1,0:T(8,128)(2,1)S(1)} %get-tuple-element.4) | data formatting | bytes 1769472
  77.5 1.0 %copy.11 = bf16[3,2,2,192,192]{4,3,2,1,0:T(8,128)(2,1)} copy(bf16[3,2,2,192,192]{4,3,2,1,0:T(8,128)(2,1)S(1)} %get-tuple-element.5) | data formatting | bytes 1769472
Async XLA Ops:
  0.6 1.3 %copy-start = (bf16[3,2,2,192,192]{4,3,2,1,0:T(8,128)(2,1)S(1)}, bf16[3,2,2,192,192]{4,3,2,1,0:T(8,128)(2,1)}, u32[]{:S(2)}) copy-start(bf16[3,2,2,192,192]{4,3,2,1,0:T(8,128)(2,1)} %s.1) | copy-start | bytes 2654212

commit v4 on v2

--- a/solution.py
+++ b/solution.py
@@ -325,16 +325,15 @@
                 for t, (i, k) in enumerate(SETS[mine]):
                     lf[e, k, pl.ds(i, CHIPS, stride=3), :] = m[mine][comb(t, e), :]
 
-        def take(mine):
-            other = 1 - mine
-            for e in range(OWN):
+        each(stage, give)
+        for e in range(OWN):
+            def take(mine):
+                other = 1 - mine
                 arrived(nr[other].at[e], NEW + OWN * other + e)
                 for t, (i, k) in enumerate(SETS[other]):
                     lf[e, k, pl.ds(i, CHIPS, stride=3), :] = nr[other][e, t].astype(F32)
 
-        each(stage, give)
-        each(stage, take)
-        for e in range(OWN):
+            each(stage, take)
             second(e, slab)
 
     for t in range(2):

time: 79 us -> 79.3 us (level)
  no operation moved by 1% of the time
where the time goes in v4:
time: 79.3 us; the launch traced here: 78.8 us
  Pallas kernels  74.8 us (94%)
  local copies, waits for them, and re-layouts  3.29 us (4%)
    pallas_call x1, Pallas kernels, shards(): pl.pallas_call(kernel, out_shape=(out, out), in_specs=[pl.BlockSpec(memor...  74.8 us
    unnamed x4, local copies, waits for them, and re-layouts  3.29 us

profile of v4, /device:TPU:1, one launch (start us, length us, event | category | flops | bytes accessed | tf_op | source)
XLA Modules:
  0.0 78.8 jit_solution(9859041465132854149)
XLA Ops:
  0.6 0.0 copy-start
  0.6 1.3 %copy-done = bf16[3,2,2,192,192]{4,3,2,1,0:T(8,128)(2,1)S(1)} copy-done((bf16[3,2,2,192,192]{4,3,2,1,0:T(8,128)(2,1)S(1)}, bf16[3,2,2,192,192]{4,3,2,1,0:T(8,128)(2,1)}, u32[]{:S(2)}) %copy-start) | copy-done | bytes 884760
  1.9 74.8 %wire.1 = (bf16[3,2,2,192,192]{4,3,2,1,0:T(8,128)(2,1)S(1)}, bf16[3,2,2,192,192]{4,3,2,1,0:T(8,128)(2,1)S(1)}) custom-call(bf16[3,2,3,2,192,192]{5,4,3,2,1,0:T(8,128)(2,1)} %g_hbm.1, bf16[3,2,2,192,192]{4,3,2,1,0:T(8,128)(2,1)S(1)} %copy-done, f32[2,2,288,384]{3,2,1,0:T(8,128)} %bitcast.1, bf16[768,768]{1,0:T(8,128)(2,1)} %constant.6.clone.tw_hbm, ...), custom_call_target="tpu_custom_call" | custom-call | tf_op jit(solution)/shard_map/wire/pallas_call | solution.py:360
  76.7 1.0 %copy.10 = bf16[3,2,2,192,192]{4,3,2,1,0:T(8,128)(2,1)} copy(bf16[3,2,2,192,192]{4,3,2,1,0:T(8,128)(2,1)S(1)} %get-tuple-element.4) | data formatting | bytes 1769472
  77.8 1.0 %copy.11 = bf16[3,2,2,192,192]{4,3,2,1,0:T(8,128)(2,1)} copy(bf16[3,2,2,192,192]{4,3,2,1,0:T(8,128)(2,1)S(1)} %get-tuple-element.5) | data formatting | bytes 1769472
Async XLA Ops:
  0.6 1.3 %copy-start = (bf16[3,2,2,192,192]{4,3,2,1,0:T(8,128)(2,1)S(1)}, bf16[3,2,2,192,192]{4,3,2,1,0:T(8,128)(2,1)}, u32[]{:S(2)}) copy-start(bf16[3,2,2,192,192]{4,3,2,1,0:T(8,128)(2,1)} %s.1) | copy-start | bytes 2654212
